TPU v7x, 32 devices: a whole 2x2x4 slice. The times are simulated.
32 devices in a mesh: groups: 2 (over x), head: 8 (over z, y), dp: 2 (over core).
Axes of the slice: x: 2, y: 2, z: 4, core: 2. Of those that a mesh axis runs over, the one named last changes fastest.
Arguments:
- head_outputs: bfloat16 [768, 8, 128], P(('groups', 'head', 'dp')), parts along dimension 0, may hold values from -91 to 91
- active: int32 [768, 8, 32], P(('groups', 'head', 'dp')), parts along dimension 0, may hold values from 0 to 8191, as said below
- enc_weight: bfloat16 [16, 8192, 128], P(('groups', 'head')), parts along dimension 0, may hold values from -0.5 to 0.5
- enc_bias: float32 [16, 8192], P(('groups', 'head')), parts along dimension 0, may hold values from -3 to 3
- dec_weight: bfloat16 [16, 8192, 128], P(('groups', 'head')), parts along dimension 0, may hold values from -1 to 1
- dec_bias: float32 [16, 128], P(('groups', 'head')), parts along dimension 0, may hold values from -3 to 3
Outputs:
- reconstruction: bfloat16 [768, 8, 128], P(('groups', 'head', 'dp')), parts along dimension 0
- explained: float32 [16], P(('groups', 'head')), parts along dimension 0
- dec_gradient: float32 [16, 8192, 128], P(('groups', 'head'), 'dp'), parts along dimension 0
There are 2 independent parts, one for each index of `groups`. A program takes and returns all parts, laid end to end along the dimension named above; each array names one. Nothing has to cross between parts.
Inputs may be any that keep to these rules, and one draw needn't show every extreme that they name: `active`: the 32 indices of one token and head lie one in each block of 256 consecutive latents, so they are distinct.
All inputs are finite; a program needn't handle non-finite values.
Results may differ from a plain program's by a relative error of at most 0.0069.
Values may be sent and summed in bfloat16 or wider, within the bound.
A program may use at most 64 MiB of HBM per device.

v0:
```python
import math

import jax
import jax.numpy as jnp
from jax import lax
from jax.sharding import PartitionSpec as P

EPSILON = 1e-06


def scatter_term(latent_codes, scaled_error, picked, offset, length):
    rows = picked.shape[0]
    block = math.gcd(rows, 512)
    features = scaled_error.shape[1]

    def add_block(index, total):
        codes_blk = lax.dynamic_slice_in_dim(latent_codes, index * block, block, 0)
        error_blk = lax.dynamic_slice_in_dim(scaled_error, index * block, block, 0)
        picked_blk = lax.dynamic_slice_in_dim(picked, index * block, block, 0)
        products = (
            codes_blk.astype(jnp.float32)[:, :, None] * error_blk.astype(jnp.float32)[:, None, :]
        )
        shifted = picked_blk - offset
        inside = (shifted >= 0) & (shifted < length)
        target = jnp.where(inside, shifted, length)
        return total.at[target].add(products, mode="drop")

    block_term = lax.fori_loop(
        0, rows // block, add_block, jnp.zeros((length, features), jnp.float32)
    )
    return lax.optimization_barrier(block_term.astype(jnp.bfloat16)).astype(jnp.float32)


def per_device(head_outputs, active, enc_weight, enc_bias, dec_weight, dec_bias):
    shards = lax.axis_size("dp")
    rows_in = lax.all_to_all(head_outputs, "head", split_axis=1, concat_axis=0, tiled=True)
    chosen = lax.all_to_all(active, "head", split_axis=1, concat_axis=0, tiled=True)
    count_rows = rows_in.shape[0]
    feature_count = rows_in.shape[2]
    total_tokens = count_rows * shards
    latents = enc_weight.shape[1]
    picks_per = chosen.shape[2]
    share_rows = latents // shards
    block = math.gcd(count_rows, 512)
    blocks = count_rows // block
    as_float = rows_in.astype(jnp.float32)
    squares, sum_rows = lax.psum(
        (jnp.sum(as_float * as_float, axis=(0, 2)), jnp.sum(as_float, axis=0)), "dp"
    )
    norm_scale = lax.rsqrt(squares / (total_tokens * feature_count) + EPSILON)
    center = sum_rows * norm_scale[:, None] / total_tokens
    factor = latents / (total_tokens * picks_per)
    scale_here = norm_scale[0]
    center_here = center[0]
    enc_mat = enc_weight[0]
    enc_vec = enc_bias[0]
    dec_mat = dec_weight[0]
    dec_vec = dec_bias[0]

    def encode_block(inputs):
        rows_blk, picked_blk = inputs
        normed = rows_blk.astype(jnp.float32) * scale_here
        encoder_in = (normed - dec_vec).astype(jnp.bfloat16)
        enc_rows = jnp.take(enc_mat, picked_blk, axis=0)
        codes_blk = jnp.einsum(
            "rd,rkd->rk", encoder_in, enc_rows, preferred_element_type=jnp.float32
        )
        codes_blk = (codes_blk + jnp.take(enc_vec, picked_blk, axis=0)).astype(jnp.bfloat16)
        dec_rows = jnp.take(dec_mat, picked_blk, axis=0)
        recon_normed = jnp.einsum(
            "rk,rkd->rd", codes_blk, dec_rows, preferred_element_type=jnp.float32
        )
        recon_normed = recon_normed + dec_vec
        rebuilt_blk = (recon_normed / scale_here).astype(jnp.bfloat16)
        mismatch = recon_normed - normed
        error_blk = (mismatch * factor).astype(jnp.bfloat16)
        return (
            rebuilt_blk,
            codes_blk,
            error_blk,
            jnp.sum(mismatch * mismatch),
            jnp.sum(jnp.square(normed - center_here)),
        )

    picked = chosen[:, 0]
    outputs = lax.map(
        encode_block,
        (
            rows_in[:, 0].reshape(blocks, block, feature_count),
            picked.reshape(blocks, block, picks_per),
        ),
    )
    rebuilt = [outputs[0].reshape(count_rows, feature_count)]
    latent_codes = outputs[1].reshape(count_rows, picks_per)
    scaled_error = outputs[2].reshape(count_rows, feature_count)
    err_terms = [jnp.sum(outputs[3])]
    var_terms = [jnp.sum(outputs[4])]
    full_term = scatter_term(latent_codes, scaled_error, picked, 0, latents)
    summed = lax.psum(full_term.astype(jnp.bfloat16), "dp").astype(jnp.float32)
    gradients = [lax.dynamic_slice_in_dim(summed, lax.axis_index("dp") * share_rows, share_rows, 0)]
    totals = lax.psum((jnp.stack(err_terms), jnp.stack(var_terms)), "dp")
    explained = 1.0 - totals[0] / totals[1]
    stacked = jnp.stack(rebuilt, axis=1)
    returned = lax.all_to_all(stacked, "head", split_axis=0, concat_axis=1, tiled=True)
    return (returned, explained, jnp.stack(gradients, axis=0))


def solution(mesh):
    placed = (
        P(("groups", "head", "dp"), None, None),
        P(("groups", "head", "dp"), None, None),
        P(("groups", "head"), None, None),
        P(("groups", "head"), None),
        P(("groups", "head"), None, None),
        P(("groups", "head"), None),
    )
    return jax.shard_map(
        per_device,
        mesh=mesh,
        in_specs=placed,
        out_specs=(
            P(("groups", "head", "dp"), None, None),
            P(("groups", "head")),
            P(("groups", "head"), "dp", None),
        ),
        check_vma=False,
    )
```

profile of v0, /device:TPU:0, one launch (start us, length us, event | category | flops | bytes accessed | tf_op | source)
XLA Modules:
  0.0 204.7 jit_solution(8415004250935383341)
XLA Ops:
  7.2 0.9 copy.33
  8.1 0.7 reshape.122
  8.8 7.3 %all-to-all-start.1 = ((s32[8,1,768]{2,1,0:T(1,128)}), s32[8,1,768]{2,1,0:T(1,128)S(1)}, u32[]{:S(2)}, u32[]{:S(2)}) async-start(s32[8,1,768]{2,1,0:T(1,128)} %reshape.122), calls=%async_computation.1 | async-start | bytes 49152 | tf_op jit(solution)/shard_map/all_to_all | solution.py:37
  16.1 1.4 copy.19
  17.5 5.2 %all-to-all-done.1 = s32[8,1,768]{2,1,0:T(1,128)S(1)} async-done(((s32[8,1,768]{2,1,0:T(1,128)}), s32[8,1,768]{2,1,0:T(1,128)S(1)}, u32[]{:S(2)}, u32[]{:S(2)}) %all-to-all-start.1) | async-done | bytes 24608 | tf_op jit(solution)/shard_map/all_to_all | solution.py:37
  22.7 3.3 %all-to-all-start = ((bf16[24,8,128]{2,0,1:T(8,128)(2,1)}), bf16[24,8,128]{2,0,1:T(8,128)(2,1)S(1)}, u32[]{:S(2)}, u32[]{:S(2)}) async-start(bf16[24,8,128]{2,0,1:T(8,128)(2,1)} %copy.19), calls=%async_computation | async-start | bytes 98304 | tf_op jit(solution)/shard_map/all_to_all | solution.py:36
  26.2 0.5 broadcast.71
  26.7 0.7 reduce.4
  27.5 5.3 %all-to-all-done = bf16[24,8,128]{2,0,1:T(8,128)(2,1)S(1)} async-done(((bf16[24,8,128]{2,0,1:T(8,128)(2,1)}), bf16[24,8,128]{2,0,1:T(8,128)(2,1)S(1)}, u32[]{:S(2)}, u32[]{:S(2)}) %all-to-all-start) | async-done | bytes 49184 | tf_op jit(solution)/shard_map/all_to_all | solution.py:36
  32.8 0.6 convert_reduce_fusion
  33.4 3.1 %all-reduce.1 = (f32[1]{0:T(128)}, f32[1,128]{1,0:T(1,128)S(1)}) all-reduce(f32[1]{0:T(128)} %bitcast.23, f32[1,128]{1,0:T(1,128)S(1)} %bitcast.141), channel_id=1, replica_groups=mesh['groups'=2,'head'=8,'dp'=2] {'dp'}, use_global_device_ids=true, to_apply=%region_1.0 | all-reduce | flops 129 | bytes 1032 | tf_op jit(solution)/shard_map/psum | solution.py:47
  37.2 87.5 %while.31 = (s32[]{:T(128)}, bf16[3,64,128]{2,1,0:T(8,128)(2,1)S(1)}, bf16[3,64,32]{2,1,0:T(8,128)(2,1)S(1)}, bf16[3,64,128]{2,1,0:T(8,128)(2,1)S(1)}, f32[3]{0:...) while((s32[]{:T(128)}, ...), condition=%wide.region_7.9_spmd, body=%wide.region_4.8_spmd.sunk | while | flops 1773568 | bytes 12164393 | solution.py:86
  37.3 7.6 %gather_fusion = bf16[2048,128]{1,0:T(8,128)(2,1)S(1)} fusion(bf16[8192,128]{1,0:T(8,128)(2,1)} %get-tuple-element.415, s32[2048]{0:T(1024)S(1)} %broadcast_clamp_fusion.4), kind=kCustom, calls=%fused_computation.1.clone.clone.1 | custom fusion | bytes 1056768 | tf_op jit(solution)/shard_map/while/body/eval_jaxpr/jit(_take)/gather | solution.py:69
  45.0 6.2 %gather_fusion.1 = bf16[2048,128]{1,0:T(8,128)(2,1)S(1)} fusion(bf16[8192,128]{1,0:T(8,128)(2,1)S(1)} %copy-done.1, s32[2048]{0:T(1024)S(1)} %broadcast_clamp_fusion.4), kind=kCustom, calls=%fused_computation.clone.clone.1 | custom fusion | bytes 1056768 | tf_op jit(solution)/shard_map/while/body/eval_jaxpr/jit(_take)/gather | solution.py:64
  51.8 11.8 %gather_fusion.2 = f32[2048]{0:T(1024)S(1)} fusion(f32[8192]{0:T(1024)S(1)} %copy-done, s32[2048]{0:T(1024)S(1)} %broadcast_clamp_fusion.5), kind=kCustom, calls=%fused_computation.2.clone.1 | custom fusion | bytes 24576 | tf_op jit(solution)/shard_map/while/body/eval_jaxpr/jit(_take)/gather | solution.py:68
  64.1 0.7 fusion.36
  64.8 0.8 dynamic_update_slice.27
  65.6 0.8 dynamic_update_slice.28
  66.5 7.6 %gather_fusion = bf16[2048,128]{1,0:T(8,128)(2,1)S(1)} fusion(bf16[8192,128]{1,0:T(8,128)(2,1)} %get-tuple-element.415, s32[2048]{0:T(1024)S(1)} %broadcast_clamp_fusion.4), kind=kCustom, calls=%fused_computation.1.clone.clone.1 | custom fusion | bytes 1056768 | tf_op jit(solution)/shard_map/while/body/eval_jaxpr/jit(_take)/gather | solution.py:69
  74.1 6.2 %gather_fusion.1 = bf16[2048,128]{1,0:T(8,128)(2,1)S(1)} fusion(bf16[8192,128]{1,0:T(8,128)(2,1)S(1)} %copy-done.1, s32[2048]{0:T(1024)S(1)} %broadcast_clamp_fusion.4), kind=kCustom, calls=%fused_computation.clone.clone.1 | custom fusion | bytes 1056768 | tf_op jit(solution)/shard_map/while/body/eval_jaxpr/jit(_take)/gather | solution.py:64
  80.9 11.8 %gather_fusion.2 = f32[2048]{0:T(1024)S(1)} fusion(f32[8192]{0:T(1024)S(1)} %copy-done, s32[2048]{0:T(1024)S(1)} %broadcast_clamp_fusion.5), kind=kCustom, calls=%fused_computation.2.clone.1 | custom fusion | bytes 24576 | tf_op jit(solution)/shard_map/while/body/eval_jaxpr/jit(_take)/gather | solution.py:68
  93.3 0.7 fusion.36
  94.0 0.8 dynamic_update_slice.27
  94.8 0.8 dynamic_update_slice.28
  95.6 7.6 %gather_fusion = bf16[2048,128]{1,0:T(8,128)(2,1)S(1)} fusion(bf16[8192,128]{1,0:T(8,128)(2,1)} %get-tuple-element.415, s32[2048]{0:T(1024)S(1)} %broadcast_clamp_fusion.4), kind=kCustom, calls=%fused_computation.1.clone.clone.1 | custom fusion | bytes 1056768 | tf_op jit(solution)/shard_map/while/body/eval_jaxpr/jit(_take)/gather | solution.py:69
  103.3 6.2 %gather_fusion.1 = bf16[2048,128]{1,0:T(8,128)(2,1)S(1)} fusion(bf16[8192,128]{1,0:T(8,128)(2,1)S(1)} %copy-done.1, s32[2048]{0:T(1024)S(1)} %broadcast_clamp_fusion.4), kind=kCustom, calls=%fused_computation.clone.clone.1 | custom fusion | bytes 1056768 | tf_op jit(solution)/shard_map/while/body/eval_jaxpr/jit(_take)/gather | solution.py:64
  109.5 0.4 fusion.33
  110.1 11.8 %gather_fusion.2 = f32[2048]{0:T(1024)S(1)} fusion(f32[8192]{0:T(1024)S(1)} %copy-done, s32[2048]{0:T(1024)S(1)} %broadcast_clamp_fusion.5), kind=kCustom, calls=%fused_computation.2.clone.1 | custom fusion | bytes 24576 | tf_op jit(solution)/shard_map/while/body/eval_jaxpr/jit(_take)/gather | solution.py:68
  122.4 0.7 fusion.36
  123.1 0.8 dynamic_update_slice.27
  123.9 0.8 dynamic_update_slice.28
  124.7 2.2 %broadcast_in_dim.56 = f32[8192,128]{1,0:T(8,128)} broadcast(f32[]{:T(128)} %constant.98.clone.1), dimensions={} | broadcast | bytes 4194308 | tf_op jit(solution)/shard_map/broadcast_in_dim | solution.py:29
  126.9 44.6 %while.32 = (s32[]{:T(128)}, f32[8192,128]{1,0:T(8,128)}, s32[192,32]{1,0:T(8,128)S(1)}, bf16[192,32]{1,0:T(8,128)(2,1)S(1)}, bf16[192,128]{1,0:T(8,128)(2,1)S(1...) while((s32[]{:T(128)}, f32[8192,128]{1,0:T(8,128)}, s32[192,32]{1,0:T(8,128)S(1)}, ...), condition=%wide.region_14.16_spmd, body=%wide.region_12.15_spmd.sunk | while | flops 548870 | bytes 4337823 | solution.py:28
  127.3 14.4 %scatter_fusion = f32[8192,128]{1,0:T(8,128)} fusion(f32[8192,128]{1,0:T(8,128)} %get-tuple-element.428, s32[2048]{0:T(1024)S(1)} %reshape.149, f32[2048,128]{1,0:T(8,128)S(1)} %bitcast.122), kind=kCustom, calls=%fused_computation.3.clone.1 | custom fusion | flops 262144 | bytes 3153920 | tf_op jit(solution)/shard_map/while/body/eval_jaxpr/scatter-add | solution.py:26
  142.2 14.4 %scatter_fusion = f32[8192,128]{1,0:T(8,128)} fusion(f32[8192,128]{1,0:T(8,128)} %get-tuple-element.428, s32[2048]{0:T(1024)S(1)} %reshape.149, f32[2048,128]{1,0:T(8,128)S(1)} %bitcast.122), kind=kCustom, calls=%fused_computation.3.clone.1 | custom fusion | flops 262144 | bytes 3153920 | tf_op jit(solution)/shard_map/while/body/eval_jaxpr/scatter-add | solution.py:26
  157.1 14.4 %scatter_fusion = f32[8192,128]{1,0:T(8,128)} fusion(f32[8192,128]{1,0:T(8,128)} %get-tuple-element.428, s32[2048]{0:T(1024)S(1)} %reshape.149, f32[2048,128]{1,0:T(8,128)S(1)} %bitcast.122), kind=kCustom, calls=%fused_computation.3.clone.1 | custom fusion | flops 262144 | bytes 3153920 | tf_op jit(solution)/shard_map/while/body/eval_jaxpr/scatter-add | solution.py:26
  171.5 3.7 %convert_element_type.47 = bf16[8192,128]{1,0:T(8,128)(2,1)} convert(f32[8192,128]{1,0:T(8,128)} %get-tuple-element.179) | non-fusion elementwise | flops 1048576 | bytes 6291456 | tf_op jit(solution)/shard_map/convert_element_type | solution.py:31
  175.2 0.5 broadcast.72
  175.7 0.7 reduce.5
  176.4 0.6 reshape.124
  177.0 3.3 %all-to-all-start.2 = ((bf16[8,2,1536]{2,1,0:T(2,128)(2,1)}), bf16[8,2,1536]{2,1,0:T(2,128)(2,1)S(1)}, u32[]{:S(2)}, u32[]{:S(2)}) async-start(bf16[8,2,1536]{2,1,0:T(2,128)(2,1)} %reshape.124), calls=%async_computation.2 | async-start | bytes 98304 | tf_op jit(solution)/shard_map/all_to_all | solution.py:104
  180.4 0.6 reduce_sum.62
  181.0 0.6 reduce_sum.63
  181.6 3.1 %all-reduce = (f32[1]{0:T(128)}, f32[1]{0:T(128)}) all-reduce(f32[1]{0:T(128)} %bitcast.35, f32[1]{0:T(128)} %bitcast.36), channel_id=1, replica_groups=mesh['groups'=2,'head'=8,'dp'=2] {'dp'}, use_global_device_ids=true, to_apply=%region_9.11 | all-reduce | flops 2 | bytes 16 | tf_op jit(solution)/shard_map/psum | solution.py:101
  186.0 1.1 all-to-all-done.2
  187.2 0.6 copy.22
  187.8 6.2 %all-reduce.4.cloned.1.call-done = bf16[8192,128]{1,0:T(8,128)(2,1)} async-done(((bf16[8192,128]{1,0:T(8,128)(2,1)}), bf16[8192,128]{1,0:T(8,128)(2,1)}) %all-reduce.4.cloned.1.call-update) | async-done | bytes 2097168 | tf_op jit(solution)/shard_map/psum | solution.py:99
  194.0 2.7 %convert_bitcast_fusion = f32[1,4096,128]{2,1,0:T(8,128)} fusion(bf16[8192,128]{1,0:T(8,128)(2,1)} %all-reduce.4.cloned.1.call-done, s32[]{:T(128)S(6)} %select_n.53), kind=kLoop, calls=%fused_computation.41 | loop fusion | flops 524288 | bytes 3145732 | tf_op jit(solution)/shard_map/stack | solution.py:105
  (79 shorter events, 4.7 us)
Async XLA Ops:
  8.8 13.9 %all-to-all-start.1 = ((s32[8,1,768]{2,1,0:T(1,128)}), s32[8,1,768]{2,1,0:T(1,128)S(1)}, u32[]{:S(2)}, u32[]{:S(2)}) async-start(s32[8,1,768]{2,1,0:T(1,128)} %reshape.122), calls=%async_computation.1 | async-start | bytes 49152 | tf_op jit(solution)/shard_map/all_to_all | solution.py:37
  22.7 10.1 %all-to-all-start = ((bf16[24,8,128]{2,0,1:T(8,128)(2,1)}), bf16[24,8,128]{2,0,1:T(8,128)(2,1)S(1)}, u32[]{:S(2)}, u32[]{:S(2)}) async-start(bf16[24,8,128]{2,0,1:T(8,128)(2,1)} %copy.19), calls=%async_computation | async-start | bytes 98304 | tf_op jit(solution)/shard_map/all_to_all | solution.py:36
  26.1 168.0 %all-reduce.4.cloned.1.call-start = ((), (), s32[]{:S(2)}) async-start(), calls=%async_computation.3 | async-start | bytes 4194304 | tf_op jit(solution)/shard_map/psum | solution.py:99
  37.3 7.6 %copy-start.1 = (bf16[8192,128]{1,0:T(8,128)(2,1)S(1)}, bf16[8192,128]{1,0:T(8,128)(2,1)}, u32[]{:S(2)}) copy-start(bf16[8192,128]{1,0:T(8,128)(2,1)} %get-tuple-element.413) | copy-start | bytes 6291460 | tf_op jit(solution)/shard_map/while
  45.0 6.2 %copy-start.2 = (f32[1,128]{1,0:T(1,128)S(1)}, f32[1,128]{1,0:T(1,128)}, u32[]{:S(2)}) copy-start(f32[1,128]{1,0:T(1,128)} %get-tuple-element.411) | copy-start | bytes 1540 | tf_op jit(solution)/shard_map/while
  45.0 6.8 %copy-start = (f32[8192]{0:T(1024)S(1)}, f32[8192]{0:T(1024)}, u32[]{:S(2)}) copy-start(f32[8192]{0:T(1024)} %get-tuple-element.414) | copy-start | bytes 98308 | tf_op jit(solution)/shard_map/while
  66.5 7.6 %copy-start.1 = (bf16[8192,128]{1,0:T(8,128)(2,1)S(1)}, bf16[8192,128]{1,0:T(8,128)(2,1)}, u32[]{:S(2)}) copy-start(bf16[8192,128]{1,0:T(8,128)(2,1)} %get-tuple-element.413) | copy-start | bytes 6291460 | tf_op jit(solution)/shard_map/while
  74.1 6.2 %copy-start.2 = (f32[1,128]{1,0:T(1,128)S(1)}, f32[1,128]{1,0:T(1,128)}, u32[]{:S(2)}) copy-start(f32[1,128]{1,0:T(1,128)} %get-tuple-element.411) | copy-start | bytes 1540 | tf_op jit(solution)/shard_map/while
  74.1 6.8 %copy-start = (f32[8192]{0:T(1024)S(1)}, f32[8192]{0:T(1024)}, u32[]{:S(2)}) copy-start(f32[8192]{0:T(1024)} %get-tuple-element.414) | copy-start | bytes 98308 | tf_op jit(solution)/shard_map/while
  95.6 7.6 %copy-start.1 = (bf16[8192,128]{1,0:T(8,128)(2,1)S(1)}, bf16[8192,128]{1,0:T(8,128)(2,1)}, u32[]{:S(2)}) copy-start(bf16[8192,128]{1,0:T(8,128)(2,1)} %get-tuple-element.413) | copy-start | bytes 6291460 | tf_op jit(solution)/shard_map/while
  103.3 6.2 %copy-start.2 = (f32[1,128]{1,0:T(1,128)S(1)}, f32[1,128]{1,0:T(1,128)}, u32[]{:S(2)}) copy-start(f32[1,128]{1,0:T(1,128)} %get-tuple-element.411) | copy-start | bytes 1540 | tf_op jit(solution)/shard_map/while
  103.3 6.8 %copy-start = (f32[8192]{0:T(1024)S(1)}, f32[8192]{0:T(1024)}, u32[]{:S(2)}) copy-start(f32[8192]{0:T(1024)} %get-tuple-element.414) | copy-start | bytes 98308 | tf_op jit(solution)/shard_map/while
  177.0 10.1 %all-to-all-start.2 = ((bf16[8,2,1536]{2,1,0:T(2,128)(2,1)}), bf16[8,2,1536]{2,1,0:T(2,128)(2,1)S(1)}, u32[]{:S(2)}, u32[]{:S(2)}) async-start(bf16[8,2,1536]{2,1,0:T(2,128)(2,1)} %reshape.124), calls=%async_computation.2 | async-start | bytes 98304 | tf_op jit(solution)/shard_map/all_to_all | solution.py:104
Sparse Core Ops, SparseCore 0:
  175.3 18.6 all-reduce.3
where the time goes:
time: 205 us
  local copies, waits for them, and re-layouts  90 us (44%)
  other arithmetic  56.4 us (28%)
  waiting for transfers between devices  17.8 us (9%)
  between operations  17.3 us (8%)
  starting transfers between devices  14 us (7%)
  blocking collectives  6.19 us (3%)
  matrix products  2.65 us (1%)
    scatter-add x3, other arithmetic, add_block(): return total.at[target].add(products, mode='drop')  43.2 us
    gather x6, local copies, waits for them, and re-layouts, encode_block(): jnp.take(enc_vec, picked_blk, axis=0)  35.6 us
    gather x3, local copies, waits for them, and re-layouts, encode_block(): dec_rows = jnp.take(dec_mat, picked_blk, axis=0)  22.8 us
    gather x3, local copies, waits for them, and re-layouts, encode_block(): enc_rows = jnp.take(enc_mat, picked_blk, axis=0)  18.6 us
    all_to_all x1, starting transfers between devices, per_device(): lax.all_to_all(active, 'head', split_axis=1, concat_axis=0, tiled=True)  7.28 us
    psum x1, waiting for transfers between devices, per_device(): summed = lax.psum(full_term.astype(jnp.bfloat16), 'dp').astype(jnp.float32)  6.2 us
    all_to_all x1, waiting for transfers between devices, per_device(): lax.all_to_all(head_outputs, 'head', split_axis=1, concat_axis=0, tiled=T...  5.32 us
    all_to_all x1, waiting for transfers between devices, per_device(): lax.all_to_all(active, 'head', split_axis=1, concat_axis=0, tiled=True)  5.2 us
  transfers between devices with their start and end apart: 4, of which 4 were waited for; matrix products, arithmetic and copies ran while one was open for 3% of the time, Pallas kernels for 0%

commit v1 on v0

v1 whole, which is shorter than its diff:
```python
import functools

import jax
import jax.numpy as jnp
from jax import lax
from jax.experimental import pallas as pl
from jax.experimental.pallas import tpu as pltpu
from jax.sharding import PartitionSpec as P

EPSILON = 1e-06
F32 = jnp.float32
BF16 = jnp.bfloat16
MESH = pl.DeviceIdType.MESH
PAD = 16


def round_up(value, unit):
    return (value + unit - 1) // unit * unit


def step_kernel(
    heads, shards, x_ref, act_ref, encw_ref, encb_ref, decw_ref, decb_ref,
    recon_ref, expl_ref, grad_ref,
    xs, acts, msg, inbox, wide, dec, dec_t, bias, codes, offs, acc, acc_in, rebuilt, reply, back, result,
    local_sem, send_a, recv_a, send_b, recv_b, send_c, recv_c,
):
    tok = x_ref.shape[0]
    feat = x_ref.shape[2]
    top = act_ref.shape[2]
    latents = encw_ref.shape[1]
    share = latents // shards
    stride = latents // top
    shift = stride.bit_length() - 1
    blocks = share // stride
    peers = heads * shards
    rows = peers * tok
    my_h = lax.axis_index("head")
    my_d = lax.axis_index("dp")
    me = my_h * shards + my_d

    first = pl.multiple_of(my_d * share, share)
    load_w = pltpu.make_async_copy(
        encw_ref.at[0, pl.ds(first, share), :], wide.at[:, pl.ds(0, feat)], local_sem.at[0]
    )
    load_d = pltpu.make_async_copy(decw_ref.at[0, pl.ds(first, share), :], dec, local_sem.at[1])
    load_b = pltpu.make_async_copy(encb_ref.at[:, pl.ds(first, share)], bias, local_sem.at[2])
    load_d.start()
    load_b.start()
    load_w.start()

    barrier = pltpu.get_barrier_semaphore()

    def greet(step, carry):
        peer = lax.rem(me + step, peers)
        pl.semaphore_signal(
            barrier, inc=1,
            device_id={"head": peer // shards, "dp": lax.rem(peer, shards)}, device_id_type=MESH,
        )
        return carry

    lax.fori_loop(1, peers, greet, 0)

    xs[...] = x_ref[...].astype(F32).reshape(tok * heads, feat)
    picked = act_ref[...].reshape(tok * heads, top)
    acts[...] = jnp.zeros_like(acts)
    acts[:, 0:top] = (picked & (stride - 1)).astype(F32)
    acts[:, top : 2 * top] = (picked >> shift).astype(F32)
    for h in range(heads):
        both = jnp.concatenate(
            [xs[pl.ds(h, tok, stride=heads), :], acts[pl.ds(h, tok, stride=heads), :]], axis=0
        )
        msg[h] = both.astype(BF16)
    pl.semaphore_wait(barrier, peers - 1)

    def copy_a(peer, slot):
        return pltpu.make_async_remote_copy(
            src_ref=msg.at[peer // shards],
            dst_ref=inbox.at[slot],
            send_sem=send_a.at[peer],
            recv_sem=recv_a.at[slot],
            device_id={"head": peer // shards, "dp": lax.rem(peer, shards)},
            device_id_type=MESH,
        )

    def send_rows(step, carry):
        copy_a(lax.rem(me + step, peers), me).start()
        return carry

    lax.fori_loop(1, peers, send_rows, 0)
    inbox[me] = msg[my_h]

    load_b.wait()
    whole = bias[...]
    high = whole.astype(BF16).astype(F32)
    mid = (whole - high).astype(BF16).astype(F32)
    low = whole - high - mid
    stacked = jnp.concatenate([high, mid, low, jnp.zeros((5, share), F32)], axis=0)
    wide[:, pl.ds(feat, feat)] = jnp.zeros((share, feat), BF16)
    wide[:, pl.ds(feat, 8)] = jnp.transpose(stacked).astype(BF16)
    load_d.wait()
    for b in range(blocks):
        dec_t[b] = jnp.transpose(dec[pl.ds(b * stride, stride), :])
    load_w.wait()

    def take_rows(step, carry):
        source = lax.rem(me + step, peers)
        copy_a(source, source).wait_recv()
        return carry

    lax.fori_loop(1, peers, take_rows, 0)

    arrived = inbox[...].astype(F32)
    x = arrived[:, 0:tok, :].reshape(rows, feat)
    index_t = jnp.transpose(arrived[:, tok : 2 * tok, :].reshape(rows, feat))
    squares = jnp.sum(jnp.sum(x * x, axis=0, keepdims=True), axis=1, keepdims=True)
    scale = lax.rsqrt(squares / (rows * feat) + EPSILON)
    normed = x * scale
    vec = decb_ref[...]
    encoder_in = (normed - vec).astype(BF16)
    ones = (lax.broadcasted_iota(jnp.int32, (rows, feat), 1) < 3).astype(F32).astype(BF16)
    joint = jnp.concatenate([encoder_in, ones], axis=1)

    wanted = (lax.broadcasted_iota(jnp.int32, (blocks, rows), 0) + my_d * blocks).astype(F32)
    found = jnp.zeros((blocks, rows), F32)
    for k in range(top):
        found = jnp.where(index_t[top + k : top + k + 1, :] == wanted, index_t[k : k + 1, :], found)
    offs[...] = found.astype(jnp.int32)

    latent = lax.broadcasted_iota(jnp.int32, (stride, rows), 0)
    acc[...] = jnp.zeros_like(acc)

    def encode(b, carry):
        here = pl.ds(pl.multiple_of(b * stride, stride), stride)
        scores = lax.dot_general(
            wide[here, :], joint, (((1,), (1,)), ((), ())), preferred_element_type=F32
        )
        block = jnp.where(latent == offs[pl.ds(b, 1), :], scores, 0.0).astype(BF16)
        codes[here, :] = block
        acc[...] += jnp.dot(dec_t[b], block, preferred_element_type=F32)
        return carry

    lax.fori_loop(0, blocks, encode, 0, unroll=2)

    partner = pltpu.make_async_remote_copy(
        src_ref=acc, dst_ref=acc_in, send_sem=send_b, recv_sem=recv_b,
        device_id={"head": my_h, "dp": 1 - my_d}, device_id_type=MESH,
    )
    partner.start()
    center = jnp.sum(x, axis=0, keepdims=True) * scale / rows
    spread = jnp.sum(jnp.square(normed - center))
    partner.wait_recv()

    recon_normed = jnp.transpose(acc[...] + acc_in[...]) + vec
    rebuilt[...] = recon_normed / scale
    for h in range(heads):
        start = pl.multiple_of((h * shards + my_d) * tok, 8)
        part = rebuilt[pl.ds(start, tok), :]
        extra = reply.shape[1] - tok
        if extra:
            part = jnp.concatenate([part, jnp.zeros((extra, feat), F32)], axis=0)
        reply[h] = part.astype(BF16)

    def copy_c(peer, slot):
        return pltpu.make_async_remote_copy(
            src_ref=reply.at[peer],
            dst_ref=back.at[slot],
            send_sem=send_c.at[peer],
            recv_sem=recv_c.at[slot],
            device_id={"head": peer, "dp": my_d},
            device_id_type=MESH,
        )

    def send_back(step, carry):
        copy_c(lax.rem(my_h + step, heads), my_h).start()
        return carry

    lax.fori_loop(1, heads, send_back, 0)
    back[my_h] = reply[my_h]

    mismatch = recon_normed - normed
    error = (mismatch * (latents / (rows * top))).astype(BF16)
    expl_ref[0] = 1.0 - jnp.sum(mismatch * mismatch) / spread

    def gradient(b, carry):
        here = pl.ds(pl.multiple_of(b * stride, stride), stride)
        grad_ref[0, here, :] = jnp.dot(codes[here, :], error, preferred_element_type=F32)
        return carry

    lax.fori_loop(0, blocks, gradient, 0, unroll=2)

    def take_back(step, carry):
        source = lax.rem(my_h + step, heads)
        copy_c(source, source).wait_recv()
        return carry

    lax.fori_loop(1, heads, take_back, 0)
    for h in range(heads):
        result[pl.ds(h, tok, stride=heads), :] = back[h].astype(F32)[0:tok, :]
    recon_ref[...] = result[...].reshape(tok, heads, feat).astype(BF16)

    partner.wait_send()

    def sent_a(step, carry):
        copy_a(lax.rem(me + step, peers), me).wait_send()
        return carry

    lax.fori_loop(1, peers, sent_a, 0)

    def sent_c(step, carry):
        copy_c(lax.rem(my_h + step, heads), my_h).wait_send()
        return carry

    lax.fori_loop(1, heads, sent_c, 0)


def per_device(heads, shards, head_outputs, active, enc_weight, enc_bias, dec_weight, dec_bias):
    tok, _, feat = head_outputs.shape
    latents = enc_weight.shape[1]
    top = active.shape[2]
    share = latents // shards
    stride = latents // top
    blocks = share // stride
    peers = heads * shards
    rows = peers * tok
    back_rows = round_up(tok, PAD)
    vmem = pl.BlockSpec(memory_space=pltpu.VMEM)
    anywhere = pl.BlockSpec(memory_space=pl.ANY)
    return pl.pallas_call(
        functools.partial(step_kernel, heads, shards),
        out_shape=(
            jax.ShapeDtypeStruct((tok, heads, feat), BF16),
            jax.ShapeDtypeStruct((1,), F32),
            jax.ShapeDtypeStruct((1, share, feat), F32),
        ),
        in_specs=[vmem, vmem, anywhere, anywhere, anywhere, vmem],
        out_specs=(vmem, pl.BlockSpec(memory_space=pltpu.SMEM), vmem),
        scratch_shapes=[
            pltpu.VMEM((tok * heads, feat), F32),
            pltpu.VMEM((tok * heads, feat), F32),
            pltpu.VMEM((heads, 2 * tok, feat), BF16),
            pltpu.VMEM((peers, 2 * tok, feat), BF16),
            pltpu.VMEM((share, 2 * feat), BF16),
            pltpu.VMEM((share, feat), BF16),
            pltpu.VMEM((blocks, feat, stride), BF16),
            pltpu.VMEM((1, share), F32),
            pltpu.VMEM((share, rows), BF16),
            pltpu.VMEM((blocks, rows), jnp.int32),
            pltpu.VMEM((feat, rows), F32),
            pltpu.VMEM((feat, rows), F32),
            pltpu.VMEM((rows, feat), F32),
            pltpu.VMEM((heads, back_rows, feat), BF16),
            pltpu.VMEM((heads, back_rows, feat), BF16),
            pltpu.VMEM((tok * heads, feat), F32),
            pltpu.SemaphoreType.DMA((3,)),
            pltpu.SemaphoreType.DMA((peers,)),
            pltpu.SemaphoreType.DMA((peers,)),
            pltpu.SemaphoreType.DMA,
            pltpu.SemaphoreType.DMA,
            pltpu.SemaphoreType.DMA((heads,)),
            pltpu.SemaphoreType.DMA((heads,)),
        ],
        compiler_params=pltpu.CompilerParams(
            collective_id=0, has_side_effects=True, vmem_limit_bytes=48 * 1024 * 1024
        ),
    )(head_outputs, active, enc_weight, enc_bias, dec_weight, dec_bias)


def solution(mesh):
    placed = (
        P(("groups", "head", "dp"), None, None),
        P(("groups", "head", "dp"), None, None),
        P(("groups", "head"), None, None),
        P(("groups", "head"), None),
        P(("groups", "head"), None, None),
        P(("groups", "head"), None),
    )
    return jax.shard_map(
        functools.partial(per_device, mesh.shape["head"], mesh.shape["dp"]),
        mesh=mesh,
        in_specs=placed,
        out_specs=(
            P(("groups", "head", "dp"), None, None),
            P(("groups", "head")),
            P(("groups", "head"), "dp", None),
        ),
        check_vma=False,
    )
```

time: 205 us -> 34.3 us (0.17)
  local copies, waits for them, and re-layouts: 90 us -> 6.63 us
  other arithmetic: 56.4 us -> 0 us
  Pallas kernels: 0 us -> 25 us
  waiting for transfers between devices: 17.8 us -> 0 us
  between operations: 17.3 us -> 2.35 us
  starting transfers between devices: 14 us -> 0 us
  blocking collectives: 6.19 us -> 0 us
  matrix products: 2.65 us -> 0 us
    gather x12 -> x0, local copies, waits for them, and re-layouts: 76.9 us -> none  [the longest x6 35.6 us: encode_block(): jnp.take(enc_vec, picked_blk, axis=0)]
    scatter-add x3 -> x0, other arithmetic: 43.2 us -> none  [add_block(): return total.at[target].add(products, mode='drop')]
    pallas_call x0 -> x1, Pallas kernels: none -> 25 us  [per_device(): pl.pallas_call(functools.partial(step_kernel, heads, shards), out_shape=(...]
    all_to_all x3 -> x0, starting transfers between devices: 14 us -> none  [the longest x1 7.28 us: per_device(): lax.all_to_all(active, 'head', split_axis=1, concat_axis=0, tiled=True)]
    all_to_all x3 -> x0, waiting for transfers between devices: 11.6 us -> none  [the longest x1 5.32 us: per_device(): lax.all_to_all(head_outputs, 'head', split_axis=1, concat_axis=0, tiled=T...]
    psum x1 -> x0, waiting for transfers between devices: 6.2 us -> none  [per_device(): summed = lax.psum(full_term.astype(jnp.bfloat16), 'dp').astype(jnp.float32)]
    psum x2 -> x0, blocking collectives: 6.19 us -> none  [the longest x1 3.11 us: per_device(): totals = lax.psum((jnp.stack(err_terms), jnp.stack(var_terms)), 'dp')]
    dynamic_update_slice x6 -> x0, local copies, waits for them, and re-layouts: 4.67 us -> none  [per_device(): lax.map(encode_block, (rows_in[:, 0].reshape(blocks, block, feature_count...]
  transfers between devices with their start and end apart: 4 -> 0, of which waited for: 4 -> 0; matrix products, arithmetic and copies ran while one was open for 3% -> 0% of each run, Pallas kernels for 0% -> 0%
where the time goes in v1:
time: 34.3 us; the launch traced here: 34 us
  Pallas kernels  25 us (73%)
  local copies, waits for them, and re-layouts  6.63 us (19%)
  between operations  2.35 us (7%)
    pallas_call x1, Pallas kernels, per_device(): pl.pallas_call(functools.partial(step_kernel, heads, shards), out_shape=(...  25 us
    unnamed x12, local copies, waits for them, and re-layouts  6.63 us

profile of v1, /device:TPU:0, one launch (start us, length us, event | category | flops | bytes accessed | tf_op | source)
XLA Modules:
  0.0 34.0 jit_solution(15875475980215248604)
XLA Ops:
  0.6 0.0 copy-start
  0.6 1.6 %copy-done = bf16[1,8192,128]{2,1,0:T(8,128)(2,1)S(1)} copy-done((bf16[1,8192,128]{2,1,0:T(8,128)(2,1)S(1)}, bf16[1,8192,128]{2,1,0:T(8,128)(2,1)}, u32[]{:S(2)}) %copy-start) | copy-done | bytes 2097176
  2.2 0.0 copy-start.1
  2.2 0.9 %copy-done.1 = s32[24,8,32]{2,1,0:T(8,128)S(1)} copy-done((s32[24,8,32]{2,1,0:T(8,128)S(1)}, s32[24,8,32]{2,1,0:T(8,128)}, u32[]{:S(2)}) %copy-start.1) | copy-done | bytes 24600
  3.1 0.0 copy-start.2
  3.1 0.8 %copy-done.2 = bf16[24,8,128]{2,1,0:T(8,128)(2,1)S(1)} copy-done((bf16[24,8,128]{2,1,0:T(8,128)(2,1)S(1)}, bf16[24,8,128]{2,1,0:T(8,128)(2,1)}, u32[]{:S(2)}) %copy-start.2) | copy-done | bytes 49176
  3.9 0.0 copy-start.3
  3.9 0.8 %copy-done.3 = f32[1,8192]{1,0:T(1,128)S(1)} copy-done((f32[1,8192]{1,0:T(1,128)S(1)}, f32[1,8192]{1,0:T(1,128)}, u32[]{:S(2)}) %copy-start.3) | copy-done | bytes 32792
  4.7 0.0 copy-start.4
  4.7 0.7 %copy-done.4 = f32[1,128]{1,0:T(1,128)S(1)} copy-done((f32[1,128]{1,0:T(1,128)S(1)}, f32[1,128]{1,0:T(1,128)}, u32[]{:S(2)}) %copy-start.4) | copy-done | bytes 536
  5.3 25.0 %shard_map.85 = (bf16[24,8,128]{2,1,0:T(8,128)(2,1)S(1)}, f32[1]{0:T(128)}, f32[1,4096,128]{2,1,0:T(8,128)S(1)}) custom-call(bf16[24,8,128]{2,1,0:T(8,128)(2,1)S(1)} %copy-done.2, s32[24,8,32]{2,1,0:T(8,128)S(1)} %copy-done.1, bf16[1,8192,128]{2,1,0:T(8,128)(2,1)S(1)} %copy-done, f32[1,8192]{1,0:T(1,128)S(1)} %copy-done.3, bf16[1,8192,128]{2,1,0:T(8,128)(2,1)} %decw_ref.1, ...), custom_call_target="tpu_custom_call" | custom-call | tf_op jit(solution)/shard_map/pallas_call | solution.py:228
  30.3 0.6 %copy.12 = bf16[24,8,128]{2,1,0:T(8,128)(2,1)} copy(bf16[24,8,128]{2,1,0:T(8,128)(2,1)S(1)} %get-tuple-element.6) | data formatting | bytes 98304
  31.5 1.3 %copy.14 = f32[1,4096,128]{2,1,0:T(8,128)} copy(f32[1,4096,128]{2,1,0:T(8,128)S(1)} %get-tuple-element.8) | data formatting | bytes 4194304
Async XLA Ops:
  0.6 1.6 %copy-start = (bf16[1,8192,128]{2,1,0:T(8,128)(2,1)S(1)}, bf16[1,8192,128]{2,1,0:T(8,128)(2,1)}, u32[]{:S(2)}) copy-start(bf16[1,8192,128]{2,1,0:T(8,128)(2,1)} %encw_ref.1) | copy-start | bytes 6291460
  2.2 0.9 %copy-start.1 = (s32[24,8,32]{2,1,0:T(8,128)S(1)}, s32[24,8,32]{2,1,0:T(8,128)}, u32[]{:S(2)}) copy-start(s32[24,8,32]{2,1,0:T(8,128)} %act_ref.1) | copy-start | bytes 73732
  3.1 0.8 %copy-start.2 = (bf16[24,8,128]{2,1,0:T(8,128)(2,1)S(1)}, bf16[24,8,128]{2,1,0:T(8,128)(2,1)}, u32[]{:S(2)}) copy-start(bf16[24,8,128]{2,1,0:T(8,128)(2,1)} %x_ref.1) | copy-start | bytes 147460
  3.9 0.8 %copy-start.3 = (f32[1,8192]{1,0:T(1,128)S(1)}, f32[1,8192]{1,0:T(1,128)}, u32[]{:S(2)}) copy-start(f32[1,8192]{1,0:T(1,128)} %encb_ref.1) | copy-start | bytes 98308
  4.7 0.7 %copy-start.4 = (f32[1,128]{1,0:T(1,128)S(1)}, f32[1,128]{1,0:T(1,128)}, u32[]{:S(2)}) copy-start(f32[1,128]{1,0:T(1,128)} %decb_ref.1) | copy-start | bytes 1540

commit v2 on v1

--- a/solution.py
+++ b/solution.py
@@ -12,6 +12,7 @@
 BF16 = jnp.bfloat16
 MESH = pl.DeviceIdType.MESH
 PAD = 16
+PARTS = 4
 
 
 def round_up(value, unit):
@@ -19,9 +20,9 @@
 
 
 def step_kernel(
-    heads, shards, x_ref, act_ref, encw_ref, encb_ref, decw_ref, decb_ref,
+    heads, shards, x_hbm, act_hbm, encw_ref, encb_ref, decw_ref, decb_hbm,
     recon_ref, expl_ref, grad_ref,
-    xs, acts, msg, inbox, wide, dec, dec_t, bias, codes, offs, acc, acc_in, rebuilt, reply, back, result,
+    x_ref, act_ref, decb_ref, xs, acts, msg, inbox, wide, dec, dec_t, bias, codes, offs, acc, acc_in, rebuilt, reply, back, result,
     local_sem, send_a, recv_a, send_b, recv_b, send_c, recv_c,
 ):
     tok = x_ref.shape[0]
@@ -44,8 +45,14 @@
     )
     load_d = pltpu.make_async_copy(decw_ref.at[0, pl.ds(first, share), :], dec, local_sem.at[1])
     load_b = pltpu.make_async_copy(encb_ref.at[:, pl.ds(first, share)], bias, local_sem.at[2])
+    load_x = pltpu.make_async_copy(x_hbm, x_ref, local_sem.at[3])
+    load_a = pltpu.make_async_copy(act_hbm, act_ref, local_sem.at[4])
+    load_v = pltpu.make_async_copy(decb_hbm, decb_ref, local_sem.at[5])
+    load_x.start()
+    load_a.start()
+    load_b.start()
+    load_v.start()
     load_d.start()
-    load_b.start()
     load_w.start()
 
     barrier = pltpu.get_barrier_semaphore()
@@ -60,6 +67,8 @@
 
     lax.fori_loop(1, peers, greet, 0)
 
+    load_x.wait()
+    load_a.wait()
     xs[...] = x_ref[...].astype(F32).reshape(tok * heads, feat)
     picked = act_ref[...].reshape(tok * heads, top)
     acts[...] = jnp.zeros_like(acts)
@@ -90,6 +99,7 @@
     inbox[me] = msg[my_h]
 
     load_b.wait()
+    load_v.wait()
     whole = bias[...]
     high = whole.astype(BF16).astype(F32)
     mid = (whole - high).astype(BF16).astype(F32)
@@ -103,7 +113,7 @@
     load_w.wait()
 
     def take_rows(step, carry):
-        source = lax.rem(me + step, peers)
+        source = lax.rem(me - step + peers, peers)
         copy_a(source, source).wait_recv()
         return carry
 
@@ -127,7 +137,6 @@
     offs[...] = found.astype(jnp.int32)
 
     latent = lax.broadcasted_iota(jnp.int32, (stride, rows), 0)
-    acc[...] = jnp.zeros_like(acc)
 
     def encode(b, carry):
         here = pl.ds(pl.multiple_of(b * stride, stride), stride)
@@ -136,10 +145,14 @@
         )
         block = jnp.where(latent == offs[pl.ds(b, 1), :], scores, 0.0).astype(BF16)
         codes[here, :] = block
-        acc[...] += jnp.dot(dec_t[b], block, preferred_element_type=F32)
-        return carry
-
-    lax.fori_loop(0, blocks, encode, 0, unroll=2)
+        return carry
+
+    lax.fori_loop(0, blocks, encode, 0, unroll=4)
+    total = jnp.dot(dec_t[0], codes[0:stride, :], preferred_element_type=F32)
+    for b in range(1, blocks):
+        here = pl.ds(b * stride, stride)
+        total += jnp.dot(dec_t[b], codes[here, :], preferred_element_type=F32)
+    acc[...] = total
 
     partner = pltpu.make_async_remote_copy(
         src_ref=acc, dst_ref=acc_in, send_sem=send_b, recv_sem=recv_b,
@@ -186,10 +199,10 @@
         grad_ref[0, here, :] = jnp.dot(codes[here, :], error, preferred_element_type=F32)
         return carry
 
-    lax.fori_loop(0, blocks, gradient, 0, unroll=2)
+    lax.fori_loop(0, blocks, gradient, 0, unroll=4)
 
     def take_back(step, carry):
-        source = lax.rem(my_h + step, heads)
+        source = lax.rem(my_h - step + heads, heads)
         copy_c(source, source).wait_recv()
         return carry
 
@@ -211,6 +224,21 @@
         return carry
 
     lax.fori_loop(1, heads, sent_c, 0)
+
+
+def store_kernel(recon_in, expl_in, grad_in, recon_ref, expl_ref, grad_ref, sems):
+    size = grad_in.shape[1] // PARTS
+    copies = [pltpu.make_async_copy(recon_in, recon_ref, sems.at[PARTS])]
+    for part in range(PARTS):
+        here = pl.ds(part * size, size)
+        copies.append(
+            pltpu.make_async_copy(grad_in.at[:, here, :], grad_ref.at[:, here, :], sems.at[part])
+        )
+    for copy in copies:
+        copy.start()
+    expl_ref[0] = expl_in[0]
+    for copy in copies:
+        copy.wait()
 
 
 def per_device(heads, shards, head_outputs, active, enc_weight, enc_bias, dec_weight, dec_bias):
@@ -224,17 +252,20 @@
     rows = peers * tok
     back_rows = round_up(tok, PAD)
     vmem = pl.BlockSpec(memory_space=pltpu.VMEM)
-    anywhere = pl.BlockSpec(memory_space=pl.ANY)
-    return pl.pallas_call(
+    hbm = pl.BlockSpec(memory_space=pltpu.HBM)
+    results = pl.pallas_call(
         functools.partial(step_kernel, heads, shards),
         out_shape=(
             jax.ShapeDtypeStruct((tok, heads, feat), BF16),
             jax.ShapeDtypeStruct((1,), F32),
             jax.ShapeDtypeStruct((1, share, feat), F32),
         ),
-        in_specs=[vmem, vmem, anywhere, anywhere, anywhere, vmem],
+        in_specs=[hbm] * 6,
         out_specs=(vmem, pl.BlockSpec(memory_space=pltpu.SMEM), vmem),
         scratch_shapes=[
+            pltpu.VMEM((tok, heads, feat), BF16),
+            pltpu.VMEM((tok, heads, top), jnp.int32),
+            pltpu.VMEM((1, feat), F32),
             pltpu.VMEM((tok * heads, feat), F32),
             pltpu.VMEM((tok * heads, feat), F32),
             pltpu.VMEM((heads, 2 * tok, feat), BF16),
@@ -251,7 +282,7 @@
             pltpu.VMEM((heads, back_rows, feat), BF16),
             pltpu.VMEM((heads, back_rows, feat), BF16),
             pltpu.VMEM((tok * heads, feat), F32),
-            pltpu.SemaphoreType.DMA((3,)),
+            pltpu.SemaphoreType.DMA((6,)),
             pltpu.SemaphoreType.DMA((peers,)),
             pltpu.SemaphoreType.DMA((peers,)),
             pltpu.SemaphoreType.DMA,
@@ -262,7 +293,19 @@
         compiler_params=pltpu.CompilerParams(
             collective_id=0, has_side_effects=True, vmem_limit_bytes=48 * 1024 * 1024
         ),
-    )(head_outputs, active, enc_weight, enc_bias, dec_weight, dec_bias)
+    )(*(
+        pltpu.with_memory_space_constraint(operand, pltpu.HBM)
+        for operand in (head_outputs, active, enc_weight, enc_bias, dec_weight, dec_bias)
+    ))
+    smem = pl.BlockSpec(memory_space=pltpu.SMEM)
+    return pl.pallas_call(
+        store_kernel,
+        out_shape=tuple(jax.ShapeDtypeStruct(r.shape, r.dtype) for r in results),
+        in_specs=[vmem, smem, vmem],
+        out_specs=(hbm, smem, hbm),
+        scratch_shapes=[pltpu.SemaphoreType.DMA((1 + PARTS,))],
+        compiler_params=pltpu.CompilerParams(vmem_limit_bytes=16 * 1024 * 1024),
+    )(*results)
 
 
 def solution(mesh):

time: 34.3 us -> 25.2 us (0.73)
  local copies, waits for them, and re-layouts: 6.63 us -> 0 us
  between operations: 2.35 us -> 0.64 us
  Pallas kernels: 25 us -> 24.4 us
    unnamed x12 -> x0, local copies, waits for them, and re-layouts: 6.63 us -> none
    pallas_call x1, Pallas kernels: 25 us -> 21.9 us  [per_device(): pl.pallas_call(functools.partial(step_kernel, heads, shards), out_shape=(...]
    pallas_call x0 -> x1, Pallas kernels: none -> 2.44 us  [per_device(): pl.pallas_call(store_kernel, out_shape=tuple((jax.ShapeDtypeStruct(r.shap...]
where the time goes in v2:
time: 25.2 us; the launch traced here: 25 us
  Pallas kernels  24.4 us (97%)
  between operations  0.64 us (3%)
    pallas_call x1, Pallas kernels, per_device(): pl.pallas_call(functools.partial(step_kernel, heads, shards), out_shape=(...  21.9 us
    pallas_call x1, Pallas kernels, per_device(): pl.pallas_call(store_kernel, out_shape=tuple((jax.ShapeDtypeStruct(r.shap...  2.44 us

profile of v2, /device:TPU:0, one launch (start us, length us, event | category | flops | bytes accessed | tf_op | source)
XLA Modules:
  0.0 25.0 jit_solution(951903771846856976)
XLA Ops:
  0.6 21.9 %shard_map.85 = (bf16[24,8,128]{2,1,0:T(8,128)(2,1)S(1)}, f32[1]{0:T(128)}, f32[1,4096,128]{2,1,0:T(8,128)S(1)}) custom-call(bf16[24,8,128]{2,1,0:T(8,128)(2,1)} %x_hbm.1, s32[24,8,32]{2,1,0:T(8,128)} %act_hbm.1, bf16[1,8192,128]{2,1,0:T(8,128)(2,1)} %encw_ref.1, f32[1,8192]{1,0:T(1,128)} %encb_ref.1, bf16[1,8192,128]{2,1,0:T(8,128)(2,1)} %decw_ref.1, ...), custom_call_target="tpu_custom_call" | custom-call | tf_op jit(solution)/shard_map/pallas_call | solution.py:256
  22.6 2.4 %shard_map.86 = (bf16[24,8,128]{2,1,0:T(8,128)(2,1)}, f32[1]{0:T(128)}, f32[1,4096,128]{2,1,0:T(8,128)}) custom-call(bf16[24,8,128]{2,1,0:T(8,128)(2,1)S(1)} %get-tuple-element.6.recon_in, f32[1]{0:T(128)} %get-tuple-element.7.expl_in, f32[1,4096,128]{2,1,0:T(8,128)S(1)} %get-tuple-element.8.grad_in), custom_call_target="tpu_custom_call" | custom-call | tf_op jit(solution)/shard_map/pallas_call | solution.py:301

commit v3 on v2

--- a/solution.py
+++ b/solution.py
@@ -23,7 +23,7 @@
     heads, shards, x_hbm, act_hbm, encw_ref, encb_ref, decw_ref, decb_hbm,
     recon_ref, expl_ref, grad_ref,
     x_ref, act_ref, decb_ref, xs, acts, msg, inbox, wide, dec, dec_t, bias, codes, offs, acc, acc_in, rebuilt, reply, back, result,
-    local_sem, send_a, recv_a, send_b, recv_b, send_c, recv_c,
+    local_sem, send_a, recv_a, send_f, send_b, recv_b, send_c, recv_c,
 ):
     tok = x_ref.shape[0]
     feat = x_ref.shape[2]
@@ -58,14 +58,16 @@
     barrier = pltpu.get_barrier_semaphore()
 
     def greet(step, carry):
-        peer = lax.rem(me + step, peers)
         pl.semaphore_signal(
             barrier, inc=1,
-            device_id={"head": peer // shards, "dp": lax.rem(peer, shards)}, device_id_type=MESH,
-        )
-        return carry
-
-    lax.fori_loop(1, peers, greet, 0)
+            device_id={"head": lax.rem(my_h + step, heads), "dp": my_d}, device_id_type=MESH,
+        )
+        return carry
+
+    lax.fori_loop(1, heads, greet, 0)
+    pl.semaphore_signal(
+        barrier, inc=1, device_id={"head": my_h, "dp": 1 - my_d}, device_id_type=MESH
+    )
 
     load_x.wait()
     load_a.wait()
@@ -79,24 +81,36 @@
             [xs[pl.ds(h, tok, stride=heads), :], acts[pl.ds(h, tok, stride=heads), :]], axis=0
         )
         msg[h] = both.astype(BF16)
-    pl.semaphore_wait(barrier, peers - 1)
-
-    def copy_a(peer, slot):
+    pl.semaphore_wait(barrier, heads)
+
+    def copy_a(peer, sender):
         return pltpu.make_async_remote_copy(
-            src_ref=msg.at[peer // shards],
+            src_ref=msg.at[peer],
+            dst_ref=inbox.at[sender * shards + my_d],
+            send_sem=send_a.at[peer],
+            recv_sem=recv_a.at[sender * shards + my_d],
+            device_id={"head": peer, "dp": my_d},
+            device_id_type=MESH,
+        )
+
+    def forward(sender, side):
+        slot = sender * shards + side
+        return pltpu.make_async_remote_copy(
+            src_ref=inbox.at[slot],
             dst_ref=inbox.at[slot],
-            send_sem=send_a.at[peer],
+            send_sem=send_f.at[sender],
             recv_sem=recv_a.at[slot],
-            device_id={"head": peer // shards, "dp": lax.rem(peer, shards)},
+            device_id={"head": my_h, "dp": 1 - my_d},
             device_id_type=MESH,
         )
 
     def send_rows(step, carry):
-        copy_a(lax.rem(me + step, peers), me).start()
-        return carry
-
-    lax.fori_loop(1, peers, send_rows, 0)
+        copy_a(lax.rem(my_h + step, heads), my_h).start()
+        return carry
+
+    lax.fori_loop(1, heads, send_rows, 0)
     inbox[me] = msg[my_h]
+    forward(my_h, my_d).start()
 
     load_b.wait()
     load_v.wait()
@@ -113,11 +127,18 @@
     load_w.wait()
 
     def take_rows(step, carry):
-        source = lax.rem(me - step + peers, peers)
+        source = lax.rem(my_h - step + heads, heads)
         copy_a(source, source).wait_recv()
-        return carry
-
-    lax.fori_loop(1, peers, take_rows, 0)
+        forward(source, my_d).start()
+        return carry
+
+    lax.fori_loop(1, heads, take_rows, 0)
+
+    def take_forwarded(step, carry):
+        forward(lax.rem(my_h - step + heads, heads), 1 - my_d).wait_recv()
+        return carry
+
+    lax.fori_loop(0, heads, take_forwarded, 0)
 
     arrived = inbox[...].astype(F32)
     x = arrived[:, 0:tok, :].reshape(rows, feat)
@@ -214,10 +235,13 @@
     partner.wait_send()
 
     def sent_a(step, carry):
-        copy_a(lax.rem(me + step, peers), me).wait_send()
-        return carry
-
-    lax.fori_loop(1, peers, sent_a, 0)
+        peer = lax.rem(my_h + step, heads)
+        copy_a(peer, my_h).wait_send()
+        forward(peer, my_d).wait_send()
+        return carry
+
+    lax.fori_loop(1, heads, sent_a, 0)
+    forward(my_h, my_d).wait_send()
 
     def sent_c(step, carry):
         copy_c(lax.rem(my_h + step, heads), my_h).wait_send()
@@ -283,8 +307,9 @@
             pltpu.VMEM((heads, back_rows, feat), BF16),
             pltpu.VMEM((tok * heads, feat), F32),
             pltpu.SemaphoreType.DMA((6,)),
+            pltpu.SemaphoreType.DMA((heads,)),
             pltpu.SemaphoreType.DMA((peers,)),
-            pltpu.SemaphoreType.DMA((peers,)),
+            pltpu.SemaphoreType.DMA((heads,)),
             pltpu.SemaphoreType.DMA,
             pltpu.SemaphoreType.DMA,
             pltpu.SemaphoreType.DMA((heads,)),

time: 25.2 us -> 24.1 us (0.956)
  Pallas kernels: 24.4 us -> 23.3 us
    pallas_call x1, Pallas kernels: 21.9 us -> 20.9 us  [per_device(): pl.pallas_call(functools.partial(step_kernel, heads, shards), out_shape=(...]
where the time goes in v3:
time: 24.1 us; the launch traced here: 24 us
  Pallas kernels  23.3 us (97%)
  between operations  0.64 us (3%)
    pallas_call x1, Pallas kernels, per_device(): pl.pallas_call(functools.partial(step_kernel, heads, shards), out_shape=(...  20.9 us
    pallas_call x1, Pallas kernels, per_device(): pl.pallas_call(store_kernel, out_shape=tuple((jax.ShapeDtypeStruct(r.shap...  2.44 us

profile of v3, /device:TPU:0, one launch (start us, length us, event | category | flops | bytes accessed | tf_op | source)
XLA Modules:
  0.0 24.0 jit_solution(2711828434797732585)
XLA Ops:
  0.6 20.9 %shard_map.85 = (bf16[24,8,128]{2,1,0:T(8,128)(2,1)S(1)}, f32[1]{0:T(128)}, f32[1,4096,128]{2,1,0:T(8,128)S(1)}) custom-call(bf16[24,8,128]{2,1,0:T(8,128)(2,1)} %x_hbm.1, s32[24,8,32]{2,1,0:T(8,128)} %act_hbm.1, bf16[1,8192,128]{2,1,0:T(8,128)(2,1)} %encw_ref.1, f32[1,8192]{1,0:T(1,128)} %encb_ref.1, bf16[1,8192,128]{2,1,0:T(8,128)(2,1)} %decw_ref.1, ...), custom_call_target="tpu_custom_call" | custom-call | tf_op jit(solution)/shard_map/pallas_call | solution.py:280
  21.5 2.4 %shard_map.86 = (bf16[24,8,128]{2,1,0:T(8,128)(2,1)}, f32[1]{0:T(128)}, f32[1,4096,128]{2,1,0:T(8,128)}) custom-call(bf16[24,8,128]{2,1,0:T(8,128)(2,1)S(1)} %get-tuple-element.6.recon_in, f32[1]{0:T(128)} %get-tuple-element.7.expl_in, f32[1,4096,128]{2,1,0:T(8,128)S(1)} %get-tuple-element.8.grad_in), custom_call_target="tpu_custom_call" | custom-call | tf_op jit(solution)/shard_map/pallas_call | solution.py:326

commit v4 on v3

--- a/solution.py
+++ b/solution.py
@@ -74,12 +74,21 @@
     xs[...] = x_ref[...].astype(F32).reshape(tok * heads, feat)
     picked = act_ref[...].reshape(tok * heads, top)
     acts[...] = jnp.zeros_like(acts)
-    acts[:, 0:top] = (picked & (stride - 1)).astype(F32)
-    acts[:, top : 2 * top] = (picked >> shift).astype(F32)
+    half = stride // 2
+    band = picked >> shift
+    inner = ((picked & (half - 1)) + half) << (band & 15)
+    code = inner.astype(F32) * jnp.where(band >= 16, 65536.0, 1.0)
+    acts[:, 0:top] = jnp.where((picked & half) != 0, -code, code)
     for h in range(heads):
-        both = jnp.concatenate(
-            [xs[pl.ds(h, tok, stride=heads), :], acts[pl.ds(h, tok, stride=heads), :]], axis=0
-        )
+        index_rows = acts[pl.ds(h, tok, stride=heads), :]
+        packed = index_rows[0:8]
+        for g in range(1, tok // 8):
+            packed += pltpu.roll(index_rows[8 * g : 8 * g + 8], g * top, 1)
+        parts = [xs[pl.ds(h, tok, stride=heads), :], packed]
+        extra = msg.shape[1] - tok - 8
+        if extra:
+            parts.append(jnp.zeros((extra, feat), F32))
+        both = jnp.concatenate(parts, axis=0)
         msg[h] = both.astype(BF16)
     pl.semaphore_wait(barrier, heads)
 
@@ -142,7 +151,13 @@
 
     arrived = inbox[...].astype(F32)
     x = arrived[:, 0:tok, :].reshape(rows, feat)
-    index_t = jnp.transpose(arrived[:, tok : 2 * tok, :].reshape(rows, feat))
+    packed_rows = arrived[:, tok : tok + 8, :].reshape(peers * 8, feat)
+    groups = [
+        (pltpu.roll(packed_rows, feat - g * top, 1) if g else packed_rows).reshape(peers, 8, feat)
+        for g in range(tok // 8)
+    ]
+    index_t = jnp.transpose(jnp.concatenate(groups, axis=1).reshape(rows, feat))[0:top, :]
+    size_t = jnp.abs(index_t)
     squares = jnp.sum(jnp.sum(x * x, axis=0, keepdims=True), axis=1, keepdims=True)
     scale = lax.rsqrt(squares / (rows * feat) + EPSILON)
     normed = x * scale
@@ -151,11 +166,19 @@
     ones = (lax.broadcasted_iota(jnp.int32, (rows, feat), 1) < 3).astype(F32).astype(BF16)
     joint = jnp.concatenate([encoder_in, ones], axis=1)
 
-    wanted = (lax.broadcasted_iota(jnp.int32, (blocks, rows), 0) + my_d * blocks).astype(F32)
+    wanted = lax.broadcasted_iota(jnp.int32, (blocks, rows), 0) + my_d * blocks
+    one = jnp.ones_like(wanted)
+    unit = (one << (wanted & 15)).astype(F32) * jnp.where(wanted >= 16, 65536.0, 1.0)
+    inverse = (one << (15 - (wanted & 15))).astype(F32) * (
+        jnp.where(wanted >= 16, 2.0**-31, 2.0**-15)
+    )
+    least, limit = unit * half, unit * stride
     found = jnp.zeros((blocks, rows), F32)
     for k in range(top):
-        found = jnp.where(index_t[top + k : top + k + 1, :] == wanted, index_t[k : k + 1, :], found)
-    offs[...] = found.astype(jnp.int32)
+        size = size_t[k : k + 1, :]
+        found = jnp.where((size >= least) & (size < limit), index_t[k : k + 1, :], found)
+    offset = jnp.abs(found) * inverse - jnp.where(found < 0, 0.0, float(half))
+    offs[...] = offset.astype(jnp.int32)
 
     latent = lax.broadcasted_iota(jnp.int32, (stride, rows), 0)
 
@@ -168,7 +191,7 @@
         codes[here, :] = block
         return carry
 
-    lax.fori_loop(0, blocks, encode, 0, unroll=4)
+    lax.fori_loop(0, blocks, encode, 0, unroll=8)
     total = jnp.dot(dec_t[0], codes[0:stride, :], preferred_element_type=F32)
     for b in range(1, blocks):
         here = pl.ds(b * stride, stride)
@@ -275,6 +298,7 @@
     peers = heads * shards
     rows = peers * tok
     back_rows = round_up(tok, PAD)
+    msg_rows = round_up(tok + 8, PAD)
     vmem = pl.BlockSpec(memory_space=pltpu.VMEM)
     hbm = pl.BlockSpec(memory_space=pltpu.HBM)
     results = pl.pallas_call(
@@ -292,8 +316,8 @@
             pltpu.VMEM((1, feat), F32),
             pltpu.VMEM((tok * heads, feat), F32),
             pltpu.VMEM((tok * heads, feat), F32),
-            pltpu.VMEM((heads, 2 * tok, feat), BF16),
-            pltpu.VMEM((peers, 2 * tok, feat), BF16),
+            pltpu.VMEM((heads, msg_rows, feat), BF16),
+            pltpu.VMEM((peers, msg_rows, feat), BF16),
             pltpu.VMEM((share, 2 * feat), BF16),
             pltpu.VMEM((share, feat), BF16),
             pltpu.VMEM((blocks, feat, stride), BF16),

time: 24.1 us -> 23.6 us (0.979)
  Pallas kernels: 23.3 us -> 22.8 us
    pallas_call x1, Pallas kernels: 20.9 us -> 20.4 us  [per_device(): pl.pallas_call(functools.partial(step_kernel, heads, shards), out_shape=(...]
where the time goes in v4:
time: 23.6 us; the launch traced here: 23.5 us
  Pallas kernels  22.8 us (97%)
  between operations  0.64 us (3%)
    pallas_call x1, Pallas kernels, per_device(): pl.pallas_call(functools.partial(step_kernel, heads, shards), out_shape=(...  20.4 us
    pallas_call x1, Pallas kernels, per_device(): pl.pallas_call(store_kernel, out_shape=tuple((jax.ShapeDtypeStruct(r.shap...  2.44 us

profile of v4, /device:TPU:0, one launch (start us, length us, event | category | flops | bytes accessed | tf_op | source)
XLA Modules:
  0.0 23.5 jit_solution(17960571408279425960)
XLA Ops:
  0.6 20.4 %shard_map.85 = (bf16[24,8,128]{2,1,0:T(8,128)(2,1)S(1)}, f32[1]{0:T(128)}, f32[1,4096,128]{2,1,0:T(8,128)S(1)}) custom-call(bf16[24,8,128]{2,1,0:T(8,128)(2,1)} %x_hbm.1, s32[24,8,32]{2,1,0:T(8,128)} %act_hbm.1, bf16[1,8192,128]{2,1,0:T(8,128)(2,1)} %encw_ref.1, f32[1,8192]{1,0:T(1,128)} %encb_ref.1, bf16[1,8192,128]{2,1,0:T(8,128)(2,1)} %decw_ref.1, ...), custom_call_target="tpu_custom_call" | custom-call | tf_op jit(solution)/shard_map/pallas_call | solution.py:304
  21.0 2.4 %shard_map.86 = (bf16[24,8,128]{2,1,0:T(8,128)(2,1)}, f32[1]{0:T(128)}, f32[1,4096,128]{2,1,0:T(8,128)}) custom-call(bf16[24,8,128]{2,1,0:T(8,128)(2,1)S(1)} %get-tuple-element.6.recon_in, f32[1]{0:T(128)} %get-tuple-element.7.expl_in, f32[1,4096,128]{2,1,0:T(8,128)S(1)} %get-tuple-element.8.grad_in), custom_call_target="tpu_custom_call" | custom-call | tf_op jit(solution)/shard_map/pallas_call | solution.py:350

commit v5 on v4

--- a/solution.py
+++ b/solution.py
@@ -13,6 +13,7 @@
 MESH = pl.DeviceIdType.MESH
 PAD = 16
 PARTS = 4
+CUTS = 4
 
 
 def round_up(value, unit):
@@ -132,7 +133,7 @@
     wide[:, pl.ds(feat, 8)] = jnp.transpose(stacked).astype(BF16)
     load_d.wait()
     for b in range(blocks):
-        dec_t[b] = jnp.transpose(dec[pl.ds(b * stride, stride), :])
+        dec_t[:, pl.ds(b * stride, stride)] = jnp.transpose(dec[pl.ds(b * stride, stride), :])
     load_w.wait()
 
     def take_rows(step, carry):
@@ -192,20 +193,24 @@
         return carry
 
     lax.fori_loop(0, blocks, encode, 0, unroll=8)
-    total = jnp.dot(dec_t[0], codes[0:stride, :], preferred_element_type=F32)
-    for b in range(1, blocks):
-        here = pl.ds(b * stride, stride)
-        total += jnp.dot(dec_t[b], codes[here, :], preferred_element_type=F32)
-    acc[...] = total
-
-    partner = pltpu.make_async_remote_copy(
-        src_ref=acc, dst_ref=acc_in, send_sem=send_b, recv_sem=recv_b,
-        device_id={"head": my_h, "dp": 1 - my_d}, device_id_type=MESH,
-    )
-    partner.start()
+    acc[...] = jnp.dot(dec_t[...], codes[...], preferred_element_type=F32)
+
+    partner = []
+    for part in range(CUTS):
+        here = pl.ds(part * (feat // CUTS), feat // CUTS)
+        partner.append(
+            pltpu.make_async_remote_copy(
+                src_ref=acc.at[here, :], dst_ref=acc_in.at[here, :],
+                send_sem=send_b.at[part], recv_sem=recv_b.at[part],
+                device_id={"head": my_h, "dp": 1 - my_d}, device_id_type=MESH,
+            )
+        )
+    for copy in partner:
+        copy.start()
     center = jnp.sum(x, axis=0, keepdims=True) * scale / rows
     spread = jnp.sum(jnp.square(normed - center))
-    partner.wait_recv()
+    for copy in partner:
+        copy.wait_recv()
 
     recon_normed = jnp.transpose(acc[...] + acc_in[...]) + vec
     rebuilt[...] = recon_normed / scale
@@ -255,7 +260,8 @@
         result[pl.ds(h, tok, stride=heads), :] = back[h].astype(F32)[0:tok, :]
     recon_ref[...] = result[...].reshape(tok, heads, feat).astype(BF16)
 
-    partner.wait_send()
+    for copy in partner:
+        copy.wait_send()
 
     def sent_a(step, carry):
         peer = lax.rem(my_h + step, heads)
@@ -320,7 +326,7 @@
             pltpu.VMEM((peers, msg_rows, feat), BF16),
             pltpu.VMEM((share, 2 * feat), BF16),
             pltpu.VMEM((share, feat), BF16),
-            pltpu.VMEM((blocks, feat, stride), BF16),
+            pltpu.VMEM((feat, share), BF16),
             pltpu.VMEM((1, share), F32),
             pltpu.VMEM((share, rows), BF16),
             pltpu.VMEM((blocks, rows), jnp.int32),
@@ -334,8 +340,8 @@
             pltpu.SemaphoreType.DMA((heads,)),
             pltpu.SemaphoreType.DMA((peers,)),
             pltpu.SemaphoreType.DMA((heads,)),
-            pltpu.SemaphoreType.DMA,
-            pltpu.SemaphoreType.DMA,
+            pltpu.SemaphoreType.DMA((CUTS,)),
+            pltpu.SemaphoreType.DMA((CUTS,)),
             pltpu.SemaphoreType.DMA((heads,)),
             pltpu.SemaphoreType.DMA((heads,)),
         ],

time: 23.6 us -> 23.7 us (level)
  no operation moved by 1% of the time
where the time goes in v5:
time: 23.7 us; the launch traced here: 23.5 us
  Pallas kernels  22.9 us (97%)
  between operations  0.64 us (3%)
    pallas_call x1, Pallas kernels, per_device(): pl.pallas_call(functools.partial(step_kernel, heads, shards), out_shape=(...  20.5 us
    pallas_call x1, Pallas kernels, per_device(): pl.pallas_call(store_kernel, out_shape=tuple((jax.ShapeDtypeStruct(r.shap...  2.44 us

profile of v5, /device:TPU:0, one launch (start us, length us, event | category | flops | bytes accessed | tf_op | source)
XLA Modules:
  0.0 23.5 jit_solution(10663944403000089748)
XLA Ops:
  0.6 20.5 %shard_map.85 = (bf16[24,8,128]{2,1,0:T(8,128)(2,1)S(1)}, f32[1]{0:T(128)}, f32[1,4096,128]{2,1,0:T(8,128)S(1)}) custom-call(bf16[24,8,128]{2,1,0:T(8,128)(2,1)} %x_hbm.1, s32[24,8,32]{2,1,0:T(8,128)} %act_hbm.1, bf16[1,8192,128]{2,1,0:T(8,128)(2,1)} %encw_ref.1, f32[1,8192]{1,0:T(1,128)} %encb_ref.1, bf16[1,8192,128]{2,1,0:T(8,128)(2,1)} %decw_ref.1, ...), custom_call_target="tpu_custom_call" | custom-call | tf_op jit(solution)/shard_map/pallas_call | solution.py:310
  21.1 2.4 %shard_map.86 = (bf16[24,8,128]{2,1,0:T(8,128)(2,1)}, f32[1]{0:T(128)}, f32[1,4096,128]{2,1,0:T(8,128)}) custom-call(bf16[24,8,128]{2,1,0:T(8,128)(2,1)S(1)} %get-tuple-element.6.recon_in, f32[1]{0:T(128)} %get-tuple-element.7.expl_in, f32[1,4096,128]{2,1,0:T(8,128)S(1)} %get-tuple-element.8.grad_in), custom_call_target="tpu_custom_call" | custom-call | tf_op jit(solution)/shard_map/pallas_call | solution.py:356
